TPU v7x, 128 devices: a whole 4x4x4 slice. The times are simulated.
128 devices in a mesh: row: 8 (over x, z_hi), col: 16 (over y, z_lo, core).
Axes of the slice: x: 4, y: 4, z: 4 (z_hi: 2, z_lo: 2; z = z_hi * 2 + z_lo), core: 2. Of those that a mesh axis runs over, the one named last changes fastest.
Arguments:
- a_tiles: bfloat16 [256, 16, 128, 128], P('col', 'row'), may hold values from -6 to 6
- a_cols: int32 [256, 16], P('col', 'row'), may hold values from 0 to 223, as said below
- b_tiles: bfloat16 [1792, 48, 128, 128], P('row', 'col'), may hold values from -0.5 to 0.5
- b_cols: int32 [1792, 48], P('row', 'col'), may hold values from 0 to 111, as said below
- c_cols: int32 [256, 32], P(None, 'col'), may hold values from 0 to 111, as said below
- keep: int32 [256, 16, 48], P(None, 'row', 'col'), may hold values from 0 to 1, as said below
Outputs:
- c_tiles: bfloat16 [256, 32, 128, 128], P('row', 'col')
Inputs may be any that keep to these rules, and one draw needn't show every extreme that they name: Within one row of a_cols, the 2 entries of one inner panel are distinct. Within one row of b_cols, the 3 entries of one column panel are distinct. Within one row of c_cols, the 2 entries of one column panel are distinct. `keep`: take the 16 rows p * 16 to p * 16 + 15, the 2 entries r * 2 to r * 2 + 1 of the second dimension and the 3 entries c * 3 to c * 3 + 2 of the third: such a block holds at most 72 ones, and in every draw there is some pair (r, c) for which all 16 such blocks hold exactly 72.
All inputs are finite; a program needn't handle non-finite values.
Results may differ from a plain program's by a relative error of at most 0.011.
Values may be sent and summed in bfloat16 or wider, within the bound.
A program may use at most 320 MiB of HBM per device.

v0:
```python
import jax
import jax.numpy as jnp
from jax import lax
from jax.sharding import PartitionSpec as P


def contribute(tiles_part, cols_part, b_tiles, b_cols, c_cols, keep):
    gathered = b_tiles[cols_part]
    target = b_cols[cols_part]
    products = jnp.einsum(
        "nsij,nstjk->nstik", tiles_part, gathered, preferred_element_type=jnp.float32
    )
    weight = ((target[..., None] == c_cols[:, None, None, :]) & (keep[..., None] == 1)).astype(
        jnp.float32
    )
    result = jnp.einsum("nstu,nstik->nuik", weight, products)
    return result


def per_device(a_tiles, a_cols, b_tiles, b_cols, c_cols, keep):
    total_rows = keep.shape[0]
    slots_kept = c_cols.shape[1]
    block_size = a_tiles.shape[2]
    empty = jnp.zeros((total_rows, slots_kept, block_size, block_size), jnp.float32)
    tiles_part = lax.all_gather(a_tiles, "col", axis=0, tiled=True)
    cols_part = lax.all_gather(a_cols, "col", axis=0, tiled=True)
    update = empty + contribute(tiles_part, cols_part, b_tiles, b_cols, c_cols, keep)
    share = lax.dynamic_update_slice_in_dim(empty, update, jnp.int32(0), 0)
    summed = lax.psum_scatter(share.astype(jnp.bfloat16), "row", scatter_dimension=0, tiled=True)
    return summed


def solution(mesh):
    placed = (
        P("col", "row", None, None),
        P("col", "row"),
        P("row", "col", None, None),
        P("row", "col"),
        P(None, "col"),
        P(None, "row", "col"),
    )
    return jax.shard_map(
        per_device,
        mesh=mesh,
        in_specs=placed,
        out_specs=P("row", "col", None, None),
        check_vma=False,
    )
```

profile of v0, /device:TPU:58, one launch (start us, length us, event | category | flops | bytes accessed | tf_op | source)
XLA Modules:
  0.0 509.7 jit_solution(14482429079883124899)
XLA Ops:
  6.5 0.0 all-gather.3.cloned.1.call-start
  6.5 0.7 all-gather.3.cloned.1.call-update
  7.3 0.0 reduce-scatter.2.cloned.1.call-start
  7.3 15.6 %all-gather = s32[16,16,2]{1,2,0:T(2,128)S(1)} all-gather(s32[1,16,2]{1,2,0:T(2,128)} %bitcast.28), channel_id=1, replica_groups=mesh['row'=8,'col'=16] {'col'}, dimensions={0}, use_global_device_ids=true | all-gather | bytes 2176 | tf_op jit(solution)/shard_map/all_gather | solution.py:26
  22.9 0.1 reshape.25
  23.0 0.1 copy.18
  23.1 0.1 reshape.6
  23.3 0.8 copy.19
  24.1 0.0 copy-start
  24.1 0.0 copy-start.1
  24.1 28.6 %gather_fusion.1 = bf16[512,3,128,128]{3,2,1,0:T(8,128)(2,1)} fusion(bf16[224,3,128,128]{3,2,1,0:T(8,128)(2,1)} %param.8, s32[1024]{0:T(1024)S(1)} %pad_clamp_fusion), kind=kCustom, calls=%fused_computation.1 | custom fusion | bytes 100665344 | tf_op jit(solution)/shard_map/gather | solution.py:8
  52.7 1.0 gather_fusion
  53.7 0.0 copy-done
  53.8 0.3 copy.21
  54.0 0.0 copy-done.1
  54.1 0.1 copy.20
  54.2 47.4 %all-gather.3.cloned.1.call-done = bf16[256,2,128,128]{3,2,1,0:T(8,128)(2,1)} async-done(((bf16[16,2,128,128]{3,2,1,0:T(8,128)(2,1)}), bf16[256,2,128,128]{3,2,1,0:T(8,128)(2,1)}) %all-gather.3.cloned.1.call-update) | async-done | bytes 16777232 | tf_op jit(solution)/shard_map/all_gather | solution.py:25
  101.6 39.2 %convolution_bitcast_fusion = bf16[256,2,3,128,128]{3,4,2,1,0:T(8,128)(2,1)} fusion(bf16[256,2,3,128,128]{4,3,2,1,0:T(8,128)(2,1)} %bitcast.26, bf16[256,2,128,128]{3,2,1,0:T(8,128)(2,1)} %all-gather.3.cloned.1.call-done), kind=kOutput, calls=%fused_computation.2 | convolution fusion | flops 6442450944 | bytes 117440512 | tf_op jit(solution)/shard_map/nsij,nstjk->nstik/dot_general | solution.py:10
  140.8 96.4 %copy.23 = bf16[256,2,3,128,128]{4,2,1,3,0:T(4,128)(2,1)} copy(bf16[256,2,3,128,128]{3,4,2,1,0:T(8,128)(2,1)} %convolution_bitcast_fusion) | data formatting | bytes 100663296 | tf_op jit(solution)/shard_map/nsij,nstjk->nstik/transpose | solution.py:10
  237.3 58.1 %bitcast_convert_fusion = bf16[256,2,128,128]{3,1,2,0:T(2,128)(2,1)} fusion(bf16[256,2,3,128,128]{4,2,1,3,0:T(4,128)(2,1)} %copy.23, pred[256,2,3]{2,1,0:T(4,128)(4,1)S(1)} %copy.21, s32[256,2]{1,0:T(8,128)S(1)} %copy.20, s32[256,2,3]{2,1,0:T(2,128)S(1)} %bitcast.27), kind=kOutput, calls=%fused_computation.3 | convolution fusion | flops 100669440 | bytes 67118592 | tf_op jit(solution)/shard_map/nstu,nstik->nuik/dot_general | solution.py:16
  295.3 15.2 %copy.24 = bf16[256,2,128,128]{3,2,1,0:T(8,128)(2,1)} copy(bf16[256,2,128,128]{3,1,2,0:T(2,128)(2,1)} %bitcast_convert_fusion) | data formatting | bytes 33554432 | tf_op jit(solution)/shard_map/convert_element_type | solution.py:29
  310.5 0.0 reduce-scatter.2.cloned.1.call-update
  310.5 192.3 %reduce-scatter.2.cloned.1.call-done = bf16[32,2,128,128]{3,2,1,0:T(8,128)(2,1)} async-done(((bf16[256,2,128,128]{3,2,1,0:T(8,128)(2,1)}), bf16[32,2,128,128]{3,2,1,0:T(8,128)(2,1)}) %reduce-scatter.2.cloned.1.call-update) | async-done | bytes 2097168 | tf_op jit(solution)/shard_map/reduce_scatter | solution.py:29
  (4 shorter events, 0.0 us)
Async XLA Ops:
  6.5 95.1 %all-gather.3.cloned.1.call-start = ((), (), s32[]{:S(2)}) async-start(), calls=%async_computation.1 | async-start | bytes 17825792 | tf_op jit(solution)/shard_map/all_gather | solution.py:25
  7.3 495.6 %reduce-scatter.2.cloned.1.call-start = ((), (), s32[]{:S(2)}) async-start(), calls=%async_computation.2 | async-start | bytes 18874368 | tf_op jit(solution)/shard_map/reduce_scatter | solution.py:29
  24.1 29.6 %copy-start = (s32[256,2,3]{0,1,2:T(2,128)S(1)}, s32[256,2,3]{0,1,2:T(2,128)}, u32[]{:S(2)}) copy-start(s32[256,2,3]{0,1,2:T(2,128)} %param.11) | copy-start | bytes 18436
  24.1 29.9 %copy-start.1 = (s32[256,2]{0,1:T(2,128)S(1)}, s32[256,2]{0,1:T(2,128)}, u32[]{:S(2)}) copy-start(s32[256,2]{0,1:T(2,128)} %param.10) | copy-start | bytes 6148
Sparse Core Ops, SparseCore 0:
  9.1 92.4 all-gather.2
  310.6 192.1 reduce-scatter.1
where the time goes:
time: 514 us; the launch traced here: 510 us
  waiting for transfers between devices  240 us (47%)
  local copies, waits for them, and re-layouts  143 us (28%)
  matrix products  97.3 us (19%)
  blocking collectives  15.6 us (3%)
  between operations  13.5 us (3%)
    reduce_scatter x1, waiting for transfers between devices, per_device(): lax.psum_scatter(share.astype(jnp.bfloat16), 'row', scatter_dimension=0,...  192 us
    transpose x1, local copies, waits for them, and re-layouts, contribute(): jnp.einsum('nsij,nstjk->nstik', tiles_part, gathered, preferred_element_t...  96.4 us
    dot_general x1, matrix products, contribute(): result = jnp.einsum('nstu,nstik->nuik', weight, products)  58.1 us
    all_gather x1, waiting for transfers between devices, per_device(): tiles_part = lax.all_gather(a_tiles, 'col', axis=0, tiled=True)  47.4 us
    dot_general x1, matrix products, contribute(): jnp.einsum('nsij,nstjk->nstik', tiles_part, gathered, preferred_element_t...  39.2 us
    gather x1, local copies, waits for them, and re-layouts, contribute(): gathered = b_tiles[cols_part]  28.6 us
    all_gather x1, blocking collectives, per_device(): cols_part = lax.all_gather(a_cols, 'col', axis=0, tiled=True)  15.6 us
    convert_element_type x1, local copies, waits for them, and re-layouts, per_device(): share.astype(jnp.bfloat16)  15.2 us
  transfers between devices with their start and end apart: 2, of which 2 were waited for; matrix products, arithmetic and copies ran while one was open for 6% of the time, Pallas kernels for 0%

commit v1 on v0

v1 whole, which is shorter than its diff:
```python
import jax
import jax.numpy as jnp
from jax import lax
from jax.experimental import pallas as pl
from jax.experimental.pallas import tpu as pltpu
from jax.sharding import PartitionSpec as P

MESH = pl.DeviceIdType.MESH
T = 128
ROWS = 16
NC = 8
NR = ROWS // NC
KP = 224
SB = 3
BLOCKS = KP * SB
B_PARTS = 8


def kernel(
    meta_ref, a_ref, b_ref, out_ref,
    w, bv, rf, rd, rz, rzz, land, cols_v, meta_s, cols_s,
    sem_a, sem_f, sem_d, sem_z, sem_zz, sem_m, sem_b, sem_own, sem_s, sem_out, send_a, send_p, send_m,
):
    row, col = lax.axis_index("row"), lax.axis_index("col")
    x, zh = row // 2, row % 2
    y, zl, k = col // 4, (col // 2) % 2, col % 2
    yp, ym, y2 = (y + 1) % 4, (y + 3) % 4, (y + 2) % 4

    def dev(xx, hh, yy, ll, kk):
        return (xx * 2 + hh, yy * 4 + ll * 2 + kk)

    sibling = dev(x, zh, y, zl, 1 - k)
    z_near = dev(x, zh, y, 1 - zl, k)
    z_far = dev(x, 1 - zh, y, zl, k)
    y_up, y_down = dev(x, zh, yp, zl, k), dev(x, zh, ym, zl, k)

    def x_dev(xx):
        return dev(xx, zh, y, zl, k)

    def remote(src, dst, send, recv, device):
        return pltpu.make_async_remote_copy(
            src_ref=src, dst_ref=dst, send_sem=send, recv_sem=recv, device_id=device, device_id_type=MESH
        )

    def landed(dst, recv):
        remote(dst, dst, send_p, recv, sibling).wait_recv()

    def chunk(slot, c):
        return w.at[slot, pl.ds(c * NR, NR)]

    part = BLOCKS // B_PARTS
    b_copies = [
        pltpu.make_async_copy(b_ref.at[pl.ds(i * part, part)], bv.at[pl.ds(i * part, part)], sem_b.at[i])
        for i in range(B_PARTS)
    ]
    q_own = y * 2 + zl
    own_copy = pltpu.make_async_copy(a_ref, w.at[q_own], sem_own)
    meta_copy = pltpu.make_async_copy(meta_ref, meta_s, sem_s)
    own_copy.start()
    meta_copy.start()
    for copy in b_copies:
        copy.start()

    barrier = pltpu.get_barrier_semaphore()
    for j in range(1, 16):
        pl.semaphore_signal(barrier, 1, device_id=(row, (col + j) % 16), device_id_type=MESH)
    for device in (x_dev((x + 1) % 4), x_dev((x + 3) % 4), z_far):
        pl.semaphore_signal(barrier, 1, device_id=device, device_id_type=MESH)
    bv[BLOCKS] = jnp.zeros((T, T), bv.dtype)
    pl.semaphore_wait(barrier, 18)

    def send_a_chunk(src, slot, c, device):
        remote(src, chunk(slot, c), send_a, sem_a.at[slot, c], device).start()

    def wait_a(slot, c):
        landed(chunk(slot, c), sem_a.at[slot, c])

    def hop0(c):
        src = a_ref.at[pl.ds(c * NR, NR)]
        send_a_chunk(src, q_own, c, y_up)
        send_a_chunk(src, q_own, c, y_down)
        send_a_chunk(src, q_own, c, z_near)
        send_a_chunk(src, 8 + q_own, c, sibling)

    def pass_on(slot, c, up=None, down=None):
        wait_a(slot, c)
        src = chunk(slot, c)
        if up is not None:
            @pl.when(up)
            def _():
                send_a_chunk(src, slot, c, y_up)
        if down is not None:
            @pl.when(down)
            def _():
                send_a_chunk(src, slot, c, y_down)
        send_a_chunk(src, 8 + slot, c, sibling)

    def hop1(c):
        slot = y * 2 + 1 - zl
        pass_on(ym * 2 + zl, c, up=c % 2 == 0)
        pass_on(yp * 2 + zl, c, down=c % 2 == 1)
        wait_a(slot, c)
        src = chunk(slot, c)
        send_a_chunk(src, slot, c, y_up)
        send_a_chunk(src, slot, c, y_down)
        send_a_chunk(src, 8 + slot, c, sibling)

    def hop2(c):
        pass_on(ym * 2 + 1 - zl, c, up=c % 2 == 0)
        pass_on(yp * 2 + 1 - zl, c, down=c % 2 == 1)
        pass_on(y2 * 2 + zl, c)

    def hop3(c):
        pass_on(y2 * 2 + 1 - zl, c)

    def z_first(c, kk):
        return (c + kk) % 4 == 0

    def way(c):
        return 1 + 2 * (c % 2)

    def p_slot(yy, ll, kk):
        same = 1 - (kk + k) % 2
        return yy * 2 + ll + 8 + 8 * same

    def r_slot(ll, kk, c):
        return (ll * 2 + kk) * NC + c

    def zz_slot(xx, kk, c):
        return xx * 4 + kk * 2 + c // 4

    def send_x(xx, ll, kk, c):
        src = chunk(p_slot(xx, ll, kk), c)
        rel = ((xx - x + 4) * way(c)) % 4
        slot = r_slot(ll, kk, c)

        @pl.when(rel == 2)
        def _():
            remote(src, rf.at[slot], send_p, sem_f.at[slot], x_dev((x + way(c)) % 4)).start()

        @pl.when(rel == 3)
        def _():
            remote(src, rd.at[1, slot], send_p, sem_d.at[1, slot], x_dev((x + 4 - way(c)) % 4)).start()

    def add_into(slot, c, *others):
        for r in range(NR):
            for u in range(2):
                total = w[slot, c * NR + r, u].astype(jnp.float32)
                for ref, index in others:
                    total = total + ref[(*index, r, u)].astype(jnp.float32)
                w[slot, c * NR + r, u] = total.astype(w.dtype)

    def multiply(yy, ll, c):
        def one(dk, carry):
            kk = (k + dk) % 2
            q = yy * 2 + ll
            a_slot, out_slot = q + 8 * dk, q + 16 - 8 * dk

            @pl.when(dk == 1)
            def _():
                wait_a(a_slot, c)

            piece = yy * 4 + ll * 2 + kk
            for r in range(NR):
                local = c * NR + r
                right = []
                for s in range(2):
                    at = cols_s[piece, local * 2 + s]
                    b_word = meta_s[1 + lax.shift_right_logical(at, 7), at & 127]
                    e = (piece * ROWS + local) * 2 + s
                    c_word = meta_s[3 + e // 128, e % 128]
                    pair = []
                    for u in range(2):
                        goal = lax.shift_right_logical(c_word, 7 * u) & 127
                        which = jnp.int32(BLOCKS)
                        for t in range(SB):
                            there = lax.shift_right_logical(b_word, 7 * t) & 127
                            kept = lax.shift_right_logical(c_word, 14 + t) & 1
                            which = jnp.where((there == goal) & (kept == 1), at * SB + t, which)
                        pair.append(bv[which])
                    right.append(jnp.concatenate(pair, axis=1))
                left = jnp.concatenate([w[a_slot, local, 0], w[a_slot, local, 1]], axis=1)
                product = jnp.dot(left, jnp.concatenate(right, axis=0), preferred_element_type=jnp.float32)
                w[out_slot, local, 0] = product[:, :T].astype(w.dtype)
                w[out_slot, local, 1] = product[:, T:].astype(w.dtype)

            first = z_first(c, kk)

            @pl.when(jnp.logical_not(first))
            def _():
                send_x(yy, ll, kk, c)

            @pl.when(first & (ll != zh))
            def _():
                slot = zz_slot(yy, kk, c)
                remote(chunk(out_slot, c), rzz.at[slot], send_p, sem_zz.at[slot], z_far).start()

            return carry

        lax.fori_loop(0, 2, one, 0)

    def z_sum(c):
        for kk in range(2):
            @pl.when(z_first(c, kk))
            def _():
                def one(j, carry):
                    xx = (x + 2 + j) % 4
                    slot = zz_slot(xx, kk, c)
                    landed(rzz.at[slot], sem_zz.at[slot])
                    add_into(p_slot(xx, zh, kk), c, (rzz, (slot,)))
                    send_x(xx, zh, kk, c)
                    return carry

                lax.fori_loop(0, 4, one, 0)

    def middle(c, ll, kk):
        xx = (x + way(c)) % 4
        slot, own = r_slot(ll, kk, c), p_slot(xx, ll, kk)
        landed(rf.at[slot], sem_f.at[slot])
        add_into(own, c, (rf, (slot,)))
        remote(chunk(own, c), rd.at[0, slot], send_p, sem_d.at[0, slot], x_dev(xx)).start()

    def arrived(ll, kk, c):
        slot = r_slot(ll, kk, c)
        for side in range(2):
            landed(rd.at[side, slot], sem_d.at[side, slot])
        return (rd, (0, slot)), (rd, (1, slot))

    def write_out(own, kk, c):
        pltpu.make_async_copy(chunk(own, c), out_ref.at[pl.ds(kk * ROWS + c * NR, NR)], sem_out).start()

    def middles(c, only_z_first):
        for j in range(2):
            ll = (zl + j) % 2
            for kk in range(2):
                if only_z_first:
                    go = z_first(c, kk) & (ll == zh)
                else:
                    go = jnp.logical_not(z_first(c, kk))

                @pl.when(go)
                def _():
                    middle(c, ll, kk)

    def to_far(c):
        for kk in range(2):
            @pl.when(jnp.logical_not(z_first(c, kk)))
            def _():
                own = p_slot(x, 1 - zh, kk)
                add_into(own, c, *arrived(1 - zh, kk, c))
                slot = kk * NC + c
                remote(chunk(own, c), rz.at[slot], send_p, sem_z.at[slot], z_far).start()

    def finish(c):
        for kk in range(2):
            own = p_slot(x, zh, kk)
            slot = kk * NC + c

            @pl.when(z_first(c, kk))
            def _():
                add_into(own, c, *arrived(zh, kk, c))
                write_out(own, kk, c)

            @pl.when(jnp.logical_not(z_first(c, kk)))
            def _():
                both = arrived(zh, kk, c)
                landed(rz.at[slot], sem_z.at[slot])
                add_into(own, c, *both, (rz, (slot,)))
                write_out(own, kk, c)

    hop0(0)
    meta_copy.wait()
    for j in range(1, 16):
        remote(meta_ref, land.at[col], send_m, sem_m.at[col], (row, (col + j) % 16)).start()
    land[col] = meta_ref[...]
    hop1(0)
    for j in range(1, 16):
        other = (col + j) % 16
        landed(land.at[other], sem_m.at[other])
    cols_v[...] = land[:, 0, :]
    cols_copy = pltpu.make_async_copy(cols_v, cols_s, sem_s)
    cols_copy.start()
    cols_copy.wait()
    own_copy.wait()
    for copy in b_copies:
        copy.wait()

    def turn(c, carry):
        now, more = c < NC, c < NC - 1

        @pl.when(now)
        def _():
            multiply(y, zl, c)
            hop2(c)

        @pl.when(more)
        def _():
            hop0(c + 1)

        @pl.when(now)
        def _():
            multiply(ym, zl, c)
            multiply(yp, zl, c)
            multiply(y, 1 - zl, c)

        @pl.when((c >= 1) & (c < NC + 1))
        def _():
            z_sum(c - 1)
            middles(c - 1, False)

        @pl.when((c >= 2) & (c < NC + 2))
        def _():
            middles(c - 2, True)

        @pl.when(now)
        def _():
            hop3(c)

        @pl.when(more)
        def _():
            hop1(c + 1)

        @pl.when(now)
        def _():
            multiply(y2, zl, c)
            multiply(ym, 1 - zl, c)
            multiply(yp, 1 - zl, c)

        @pl.when((c >= 2) & (c < NC + 2))
        def _():
            to_far(c - 2)

        @pl.when(now)
        def _():
            multiply(y2, 1 - zl, c)

        @pl.when(c >= 3)
        def _():
            finish(c - 3)

        return carry

    lax.fori_loop(0, NC + 3, turn, 0)

    remote(w.at[pl.ds(0, 15)], w.at[pl.ds(0, 15)], send_a, send_a, sibling).wait_send()
    remote(w.at[pl.ds(0, 14)], w.at[pl.ds(0, 14)], send_p, send_p, sibling).wait_send()
    remote(land.at[pl.ds(0, 15)], land.at[pl.ds(0, 15)], send_m, send_m, sibling).wait_send()
    pltpu.make_async_copy(w.at[pl.ds(0, 2)], w.at[pl.ds(0, 2)], sem_out).wait()


def per_device(a_tiles, a_cols, b_tiles, b_cols, c_cols, keep):
    bf16, i32 = jnp.bfloat16, jnp.int32
    b_words = b_cols[:, 0] + 128 * b_cols[:, 1] + 16384 * b_cols[:, 2]
    kept = keep[:, :, 0] + 2 * keep[:, :, 1] + 4 * keep[:, :, 2]
    c_words = (c_cols[:, 0] + 128 * c_cols[:, 1])[:, None] + 16384 * kept
    meta = jnp.concatenate(
        [
            jnp.pad(a_cols.reshape(-1), (0, 128 - 2 * ROWS)),
            jnp.pad(b_words, (0, 256 - KP)),
            c_words.reshape(-1),
            jnp.zeros((128,), i32),
        ]
    ).reshape(8, 128)
    chunk = (NR, 2, T, T)
    vmem = pltpu.VMEM
    dma = pltpu.SemaphoreType.DMA
    return pl.pallas_call(
        kernel,
        out_shape=jax.ShapeDtypeStruct((2 * ROWS, 2, T, T), bf16),
        in_specs=[
            pl.BlockSpec(memory_space=pltpu.VMEM),
            pl.BlockSpec(memory_space=pl.ANY),
            pl.BlockSpec(memory_space=pl.ANY),
        ],
        out_specs=pl.BlockSpec(memory_space=pl.ANY),
        scratch_shapes=[
            vmem((24, ROWS, 2, T, T), bf16),
            vmem((BLOCKS + 1, T, T), bf16),
            vmem((4 * NC, *chunk), bf16),
            vmem((2, 4 * NC, *chunk), bf16),
            vmem((2 * NC, *chunk), bf16),
            vmem((16, *chunk), bf16),
            vmem((16, 8, 128), i32),
            vmem((16, 128), i32),
            pltpu.SMEM((8, 128), i32),
            pltpu.SMEM((16, 128), i32),
            dma((16, NC)),
            dma((4 * NC,)),
            dma((2, 4 * NC)),
            dma((2 * NC,)),
            dma((16,)),
            dma((16,)),
            dma((B_PARTS,)),
            dma,
            dma,
            dma,
            dma,
            dma,
            dma,
        ],
        compiler_params=pltpu.CompilerParams(
            collective_id=0, has_side_effects=True, vmem_limit_bytes=63 << 20
        ),
        cost_estimate=pl.CostEstimate(
            flops=2 * 256 * 2 * T * 2 * T * T, bytes_accessed=26 << 20, transcendentals=0
        ),
    )(meta, a_tiles, b_tiles.reshape(BLOCKS, T, T))


def solution(mesh):
    placed = (
        P("col", "row", None, None),
        P("col", "row"),
        P("row", "col", None, None),
        P("row", "col"),
        P(None, "col"),
        P(None, "row", "col"),
    )
    return jax.shard_map(
        per_device,
        mesh=mesh,
        in_specs=placed,
        out_specs=P("row", "col", None, None),
        check_vma=False,
    )
```

time: 514 us -> 169 us (0.33)
  the two profiles are of different devices: /device:TPU:58 before, /device:TPU:8 now
where the time goes in v1:
time: 169 us
  Pallas kernels  162 us (96%)
  local copies, waits for them, and re-layouts  4.52 us (3%)
  other arithmetic  2.89 us (2%)
    pallas_call x1, Pallas kernels, per_device(): pl.pallas_call(kernel, out_shape=jax.ShapeDtypeStruct((2 * ROWS, 2, T, T)...  162 us
    unnamed x2, local copies, waits for them, and re-layouts  3.91 us

profile of v1, /device:TPU:8, one launch (start us, length us, event | category | flops | bytes accessed | tf_op | source)
XLA Modules:
  0.0 169.1 jit_solution(567474279766716725)
XLA Ops:
  0.0 0.8 multiply_add_fusion.1
  0.8 0.8 multiply_add_fusion
  1.6 0.7 add_multiply_fusion
  2.3 0.8 copy.8
  3.0 0.1 reshape.28
  3.1 0.1 copy.9
  3.3 0.1 mul.59
  3.4 0.1 add.46
  3.5 0.1 add.47
  3.7 0.6 fusion.2.meta_ref
  4.3 161.7 %shard_map.64 = bf16[32,2,128,128]{3,2,1,0:T(8,128)(2,1)} custom-call(s32[8,128]{1,0:T(8,128)} %fusion.2.meta_ref, bf16[16,2,128,128]{3,2,1,0:T(8,128)(2,1)} %a_ref.1, bf16[672,128,128]{2,1,0:T(8,128)(2,1)} %bitcast.7), custom_call_target="tpu_custom_call" | custom-call | flops 4294967296 | bytes 27262976 | tf_op jit(solution)/shard_map/pallas_call | solution.py:367
  166.0 3.2 %copy.11 = bf16[32,2,128,128]{3,2,1,0:T(8,128)(2,1)} copy(bf16[32,2,128,128]{3,2,1,0:T(8,128)(2,1)} %shard_map.64) | data formatting | bytes 4194304
  (2 shorter events, 0.0 us)

commit v2 on v1

--- a/solution.py
+++ b/solution.py
@@ -8,12 +8,13 @@
 MESH = pl.DeviceIdType.MESH
 T = 128
 ROWS = 16
-NC = 8
+NC = 16
 NR = ROWS // NC
 KP = 224
 SB = 3
 BLOCKS = KP * SB
 B_PARTS = 8
+Z_FIRST = 5
 
 
 def kernel(
@@ -97,8 +98,8 @@
 
     def hop1(c):
         slot = y * 2 + 1 - zl
-        pass_on(ym * 2 + zl, c, up=c % 2 == 0)
-        pass_on(yp * 2 + zl, c, down=c % 2 == 1)
+        pass_on(ym * 2 + zl, c, up=(c + k) % 2 == 0)
+        pass_on(yp * 2 + zl, c, down=(c + k) % 2 == 1)
         wait_a(slot, c)
         src = chunk(slot, c)
         send_a_chunk(src, slot, c, y_up)
@@ -106,18 +107,18 @@
         send_a_chunk(src, 8 + slot, c, sibling)
 
     def hop2(c):
-        pass_on(ym * 2 + 1 - zl, c, up=c % 2 == 0)
-        pass_on(yp * 2 + 1 - zl, c, down=c % 2 == 1)
+        pass_on(ym * 2 + 1 - zl, c, up=(c + k) % 2 == 0)
+        pass_on(yp * 2 + 1 - zl, c, down=(c + k) % 2 == 1)
         pass_on(y2 * 2 + zl, c)
 
     def hop3(c):
         pass_on(y2 * 2 + 1 - zl, c)
 
     def z_first(c, kk):
-        return (c + kk) % 4 == 0
-
-    def way(c):
-        return 1 + 2 * (c % 2)
+        return (c + 2 * kk) % 4 == 0
+
+    def way(c, kk):
+        return 1 + 2 * ((c + kk) % 2)
 
     def p_slot(yy, ll, kk):
         same = 1 - (kk + k) % 2
@@ -127,20 +128,20 @@
         return (ll * 2 + kk) * NC + c
 
     def zz_slot(xx, kk, c):
-        return xx * 4 + kk * 2 + c // 4
+        return (xx * 2 + kk) * 4 + c // 4
 
     def send_x(xx, ll, kk, c):
         src = chunk(p_slot(xx, ll, kk), c)
-        rel = ((xx - x + 4) * way(c)) % 4
+        rel = ((xx - x + 4) * way(c, kk)) % 4
         slot = r_slot(ll, kk, c)
 
         @pl.when(rel == 2)
         def _():
-            remote(src, rf.at[slot], send_p, sem_f.at[slot], x_dev((x + way(c)) % 4)).start()
+            remote(src, rf.at[slot], send_p, sem_f.at[slot], x_dev((x + way(c, kk)) % 4)).start()
 
         @pl.when(rel == 3)
         def _():
-            remote(src, rd.at[1, slot], send_p, sem_d.at[1, slot], x_dev((x + 4 - way(c)) % 4)).start()
+            remote(src, rd.at[1, slot], send_p, sem_d.at[1, slot], x_dev((x + 4 - way(c, kk)) % 4)).start()
 
     def add_into(slot, c, *others):
         for r in range(NR):
@@ -150,50 +151,63 @@
                     total = total + ref[(*index, r, u)].astype(jnp.float32)
                 w[slot, c * NR + r, u] = total.astype(w.dtype)
 
-    def multiply(yy, ll, c):
+    def multiply(c, *places):
         def one(dk, carry):
             kk = (k + dk) % 2
-            q = yy * 2 + ll
-            a_slot, out_slot = q + 8 * dk, q + 16 - 8 * dk
+            slots = [(yy * 2 + ll + 8 * dk, yy * 2 + ll + 16 - 8 * dk) for yy, ll in places]
 
             @pl.when(dk == 1)
             def _():
-                wait_a(a_slot, c)
-
-            piece = yy * 4 + ll * 2 + kk
-            for r in range(NR):
-                local = c * NR + r
-                right = []
-                for s in range(2):
-                    at = cols_s[piece, local * 2 + s]
-                    b_word = meta_s[1 + lax.shift_right_logical(at, 7), at & 127]
-                    e = (piece * ROWS + local) * 2 + s
-                    c_word = meta_s[3 + e // 128, e % 128]
-                    pair = []
-                    for u in range(2):
-                        goal = lax.shift_right_logical(c_word, 7 * u) & 127
-                        which = jnp.int32(BLOCKS)
-                        for t in range(SB):
-                            there = lax.shift_right_logical(b_word, 7 * t) & 127
-                            kept = lax.shift_right_logical(c_word, 14 + t) & 1
-                            which = jnp.where((there == goal) & (kept == 1), at * SB + t, which)
-                        pair.append(bv[which])
-                    right.append(jnp.concatenate(pair, axis=1))
-                left = jnp.concatenate([w[a_slot, local, 0], w[a_slot, local, 1]], axis=1)
-                product = jnp.dot(left, jnp.concatenate(right, axis=0), preferred_element_type=jnp.float32)
-                w[out_slot, local, 0] = product[:, :T].astype(w.dtype)
-                w[out_slot, local, 1] = product[:, T:].astype(w.dtype)
+                for a_slot, _ in slots:
+                    wait_a(a_slot, c)
+
+            rows = [c * NR + r for r in range(NR)]
+            found = []
+            for yy, ll in places:
+                piece = yy * 4 + ll * 2 + kk
+                for local in rows:
+                    for s in range(2):
+                        at = cols_s[piece, local * 2 + s]
+                        b_word = meta_s[1 + lax.shift_right_logical(at, 7), at & 127]
+                        e = (piece * ROWS + local) * 2 + s
+                        c_word = meta_s[3 + e // 128, e % 128]
+                        for u in range(2):
+                            goal = lax.shift_right_logical(c_word, 7 * u) & 127
+                            which = jnp.int32(BLOCKS)
+                            for t in range(SB):
+                                there = lax.shift_right_logical(b_word, 7 * t) & 127
+                                kept = lax.shift_right_logical(c_word, 14 + t) & 1
+                                which = jnp.where((there == goal) & (kept == 1), at * SB + t, which)
+                            found.append(which)
+            products = []
+            for a_slot, _ in slots:
+                for local in rows:
+                    n = 4 * len(products)
+                    right = [bv[which] for which in found[n : n + 4]]
+                    right = [jnp.concatenate(right[i : i + 2], axis=1) for i in (0, 2)]
+                    left = jnp.concatenate([w[a_slot, local, 0], w[a_slot, local, 1]], axis=1)
+                    products.append(
+                        jnp.dot(left, jnp.concatenate(right, axis=0), preferred_element_type=jnp.float32)
+                    )
+            for i, (_, out_slot) in enumerate(slots):
+                for r, local in enumerate(rows):
+                    product = products[i * NR + r]
+                    w[out_slot, local, 0] = product[:, :T].astype(w.dtype)
+                    w[out_slot, local, 1] = product[:, T:].astype(w.dtype)
 
             first = z_first(c, kk)
 
             @pl.when(jnp.logical_not(first))
             def _():
-                send_x(yy, ll, kk, c)
-
-            @pl.when(first & (ll != zh))
-            def _():
-                slot = zz_slot(yy, kk, c)
-                remote(chunk(out_slot, c), rzz.at[slot], send_p, sem_zz.at[slot], z_far).start()
+                for yy, ll in places:
+                    send_x(yy, ll, kk, c)
+
+            for (yy, ll), (_, out_slot) in zip(places, slots):
+
+                @pl.when(first & (ll != zh))
+                def _():
+                    slot = zz_slot(yy, kk, c)
+                    remote(chunk(out_slot, c), rzz.at[slot], send_p, sem_zz.at[slot], z_far).start()
 
             return carry
 
@@ -214,7 +228,7 @@
                 lax.fori_loop(0, 4, one, 0)
 
     def middle(c, ll, kk):
-        xx = (x + way(c)) % 4
+        xx = (x + way(c, kk)) % 4
         slot, own = r_slot(ll, kk, c), p_slot(xx, ll, kk)
         landed(rf.at[slot], sem_f.at[slot])
         add_into(own, c, (rf, (slot,)))
@@ -273,6 +287,7 @@
     for j in range(1, 16):
         remote(meta_ref, land.at[col], send_m, sem_m.at[col], (row, (col + j) % 16)).start()
     land[col] = meta_ref[...]
+    hop0(1)
     hop1(0)
     for j in range(1, 16):
         other = (col + j) % 16
@@ -285,62 +300,62 @@
     for copy in b_copies:
         copy.wait()
 
-    def turn(c, carry):
-        now, more = c < NC, c < NC - 1
-
-        @pl.when(now)
-        def _():
-            multiply(y, zl, c)
-            hop2(c)
-
-        @pl.when(more)
-        def _():
-            hop0(c + 1)
-
-        @pl.when(now)
-        def _():
-            multiply(ym, zl, c)
-            multiply(yp, zl, c)
-            multiply(y, 1 - zl, c)
-
-        @pl.when((c >= 1) & (c < NC + 1))
-        def _():
-            z_sum(c - 1)
-            middles(c - 1, False)
-
-        @pl.when((c >= 2) & (c < NC + 2))
-        def _():
-            middles(c - 2, True)
-
-        @pl.when(now)
-        def _():
-            hop3(c)
-
-        @pl.when(more)
-        def _():
-            hop1(c + 1)
-
-        @pl.when(now)
-        def _():
-            multiply(y2, zl, c)
-            multiply(ym, 1 - zl, c)
-            multiply(yp, 1 - zl, c)
-
-        @pl.when((c >= 2) & (c < NC + 2))
-        def _():
-            to_far(c - 2)
-
-        @pl.when(now)
-        def _():
-            multiply(y2, 1 - zl, c)
-
-        @pl.when(c >= 3)
-        def _():
-            finish(c - 3)
+    def during(c, end):
+        return pl.when((c >= 0) & (c < end))
+
+    def turn(a, carry):
+        @during(a, NC)
+        def _():
+            multiply(a, (y, zl))
+
+        @during(a + 1, NC)
+        def _():
+            hop1(a + 1)
+
+        @during(a, NC)
+        def _():
+            hop2(a)
+
+        @during(a - 1, NC)
+        def _():
+            hop3(a - 1)
+
+        @during(a + 2, NC)
+        def _():
+            hop0(a + 2)
+
+        @during(a, NC)
+        def _():
+            multiply(a, (ym, zl), (yp, zl), (y, 1 - zl))
+
+        @during(a - 2, NC)
+        def _():
+            z_sum(a - 2)
+            middles(a - 2, False)
+
+        @during(a - 3, NC)
+        def _():
+            middles(a - 3, True)
+
+        @during(a, NC)
+        def _():
+            multiply(a, (y2, zl), (ym, 1 - zl), (yp, 1 - zl))
+
+        @during(a - 1, NC)
+        def _():
+            multiply(a - 1, (y2, 1 - zl))
+
+        @during(a - 3, NC)
+        def _():
+            to_far(a - 3)
+
+        @during(a - 4, NC)
+        def _():
+            finish(a - 4)
 
         return carry
 
-    lax.fori_loop(0, NC + 3, turn, 0)
+    lax.fori_loop(0, NC + 4, turn, 0)
 
     remote(w.at[pl.ds(0, 15)], w.at[pl.ds(0, 15)], send_a, send_a, sibling).wait_send()
     remote(w.at[pl.ds(0, 14)], w.at[pl.ds(0, 14)], send_p, send_p, sibling).wait_send()
@@ -379,7 +394,7 @@
             vmem((4 * NC, *chunk), bf16),
             vmem((2, 4 * NC, *chunk), bf16),
             vmem((2 * NC, *chunk), bf16),
-            vmem((16, *chunk), bf16),
+            vmem((8 * Z_FIRST, *chunk), bf16),
             vmem((16, 8, 128), i32),
             vmem((16, 128), i32),
             pltpu.SMEM((8, 128), i32),
@@ -388,7 +403,7 @@
             dma((4 * NC,)),
             dma((2, 4 * NC)),
             dma((2 * NC,)),
-            dma((16,)),
+            dma((8 * Z_FIRST,)),
             dma((16,)),
             dma((B_PARTS,)),
             dma,

time: 169 us -> 159 us (0.941)
  the two profiles are of different devices: /device:TPU:8 before, /device:TPU:58 now
where the time goes in v2:
time: 159 us
  Pallas kernels  151 us (95%)
  local copies, waits for them, and re-layouts  4.52 us (3%)
  other arithmetic  2.89 us (2%)
    pallas_call x1, Pallas kernels, per_device(): pl.pallas_call(kernel, out_shape=jax.ShapeDtypeStruct((2 * ROWS, 2, T, T)...  151 us
    unnamed x2, local copies, waits for them, and re-layouts  3.91 us

profile of v2, /device:TPU:58, one launch (start us, length us, event | category | flops | bytes accessed | tf_op | source)
XLA Modules:
  0.0 158.7 jit_solution(8198886342331152086)
XLA Ops:
  0.0 0.8 multiply_add_fusion.1
  0.8 0.8 multiply_add_fusion
  1.6 0.7 add_multiply_fusion
  2.3 0.8 copy.8
  3.0 0.1 reshape.28
  3.1 0.1 copy.9
  3.3 0.1 mul.59
  3.4 0.1 add.46
  3.5 0.1 add.47
  3.7 0.6 fusion.2.meta_ref
  4.3 151.3 %shard_map.64 = bf16[32,2,128,128]{3,2,1,0:T(8,128)(2,1)} custom-call(s32[8,128]{1,0:T(8,128)} %fusion.2.meta_ref, bf16[16,2,128,128]{3,2,1,0:T(8,128)(2,1)} %a_ref.1, bf16[672,128,128]{2,1,0:T(8,128)(2,1)} %bitcast.7), custom_call_target="tpu_custom_call" | custom-call | flops 4294967296 | bytes 27262976 | tf_op jit(solution)/shard_map/pallas_call | solution.py:382
  155.6 3.2 %copy.11 = bf16[32,2,128,128]{3,2,1,0:T(8,128)(2,1)} copy(bf16[32,2,128,128]{3,2,1,0:T(8,128)(2,1)} %shard_map.64) | data formatting | bytes 4194304
  (2 shorter events, 0.0 us)

commit v3 on v2

--- a/solution.py
+++ b/solution.py
@@ -14,13 +14,12 @@
 SB = 3
 BLOCKS = KP * SB
 B_PARTS = 8
-Z_FIRST = 5
 
 
 def kernel(
-    meta_ref, a_ref, b_ref, out_ref,
-    w, bv, rf, rd, rz, rzz, land, cols_v, meta_s, cols_s,
-    sem_a, sem_f, sem_d, sem_z, sem_zz, sem_m, sem_b, sem_own, sem_s, sem_out, send_a, send_p, send_m,
+    a_cols_ref, b_cols_ref, c_cols_ref, keep_ref, a_ref, b_ref, out_ref,
+    w, bv, rf, rd, rz, rzz, mine, land, cols_v, b_words, c_words, b_words_s, c_words_s, cols_s,
+    sem_a, sem_f, sem_d, sem_z, sem_zz, sem_m, sem_b, sem_own, sem_words, sem_cols, sem_out, send_a, send_p, send_m,
 ):
     row, col = lax.axis_index("row"), lax.axis_index("col")
     x, zh = row // 2, row % 2
@@ -56,11 +55,9 @@
     ]
     q_own = y * 2 + zl
     own_copy = pltpu.make_async_copy(a_ref, w.at[q_own], sem_own)
-    meta_copy = pltpu.make_async_copy(meta_ref, meta_s, sem_s)
-    own_copy.start()
-    meta_copy.start()
     for copy in b_copies:
         copy.start()
+    own_copy.start()
 
     barrier = pltpu.get_barrier_semaphore()
     for j in range(1, 16):
@@ -68,6 +65,18 @@
     for device in (x_dev((x + 1) % 4), x_dev((x + 3) % 4), z_far):
         pl.semaphore_signal(barrier, 1, device_id=device, device_id_type=MESH)
     bv[BLOCKS] = jnp.zeros((T, T), bv.dtype)
+    mine[...] = jnp.zeros_like(mine)
+    mine[0:2, 0:ROWS] = a_cols_ref[...]
+    b_words[0:1, 0:KP] = b_cols_ref[0:1] + 128 * b_cols_ref[1:2] + 16384 * b_cols_ref[2:3]
+    c_words[...] = (
+        c_cols_ref[0:1] + 128 * c_cols_ref[1:2] + 16384 * (keep_ref[0] + 2 * keep_ref[1] + 4 * keep_ref[2])
+    )
+    words_copies = [
+        pltpu.make_async_copy(b_words, b_words_s, sem_words.at[0]),
+        pltpu.make_async_copy(c_words, c_words_s, sem_words.at[1]),
+    ]
+    for copy in words_copies:
+        copy.start()
     pl.semaphore_wait(barrier, 18)
 
     def send_a_chunk(src, slot, c, device):
@@ -167,10 +176,9 @@
                 piece = yy * 4 + ll * 2 + kk
                 for local in rows:
                     for s in range(2):
-                        at = cols_s[piece, local * 2 + s]
-                        b_word = meta_s[1 + lax.shift_right_logical(at, 7), at & 127]
-                        e = (piece * ROWS + local) * 2 + s
-                        c_word = meta_s[3 + e // 128, e % 128]
+                        at = cols_s[16 * s + piece, local]
+                        b_word = b_words_s[0, at]
+                        c_word = c_words_s[s, piece * ROWS + local]
                         for u in range(2):
                             goal = lax.shift_right_logical(c_word, 7 * u) & 127
                             which = jnp.int32(BLOCKS)
@@ -283,19 +291,20 @@
                 write_out(own, kk, c)
 
     hop0(0)
-    meta_copy.wait()
     for j in range(1, 16):
-        remote(meta_ref, land.at[col], send_m, sem_m.at[col], (row, (col + j) % 16)).start()
-    land[col] = meta_ref[...]
+        remote(mine, land.at[col], send_m, sem_m.at[col], (row, (col + j) % 16)).start()
+    land[col] = mine[...]
     hop0(1)
     hop1(0)
     for j in range(1, 16):
         other = (col + j) % 16
         landed(land.at[other], sem_m.at[other])
-    cols_v[...] = land[:, 0, :]
-    cols_copy = pltpu.make_async_copy(cols_v, cols_s, sem_s)
+    for s in range(2):
+        cols_v[16 * s : 16 * s + 16] = land[:, s, :]
+    cols_copy = pltpu.make_async_copy(cols_v, cols_s, sem_cols)
     cols_copy.start()
-    cols_copy.wait()
+    for copy in (*words_copies, cols_copy):
+        copy.wait()
     own_copy.wait()
     for copy in b_copies:
         copy.wait()
@@ -365,17 +374,6 @@
 
 def per_device(a_tiles, a_cols, b_tiles, b_cols, c_cols, keep):
     bf16, i32 = jnp.bfloat16, jnp.int32
-    b_words = b_cols[:, 0] + 128 * b_cols[:, 1] + 16384 * b_cols[:, 2]
-    kept = keep[:, :, 0] + 2 * keep[:, :, 1] + 4 * keep[:, :, 2]
-    c_words = (c_cols[:, 0] + 128 * c_cols[:, 1])[:, None] + 16384 * kept
-    meta = jnp.concatenate(
-        [
-            jnp.pad(a_cols.reshape(-1), (0, 128 - 2 * ROWS)),
-            jnp.pad(b_words, (0, 256 - KP)),
-            c_words.reshape(-1),
-            jnp.zeros((128,), i32),
-        ]
-    ).reshape(8, 128)
     chunk = (NR, 2, T, T)
     vmem = pltpu.VMEM
     dma = pltpu.SemaphoreType.DMA
@@ -383,7 +381,7 @@
         kernel,
         out_shape=jax.ShapeDtypeStruct((2 * ROWS, 2, T, T), bf16),
         in_specs=[
-            pl.BlockSpec(memory_space=pltpu.VMEM),
+            *[pl.BlockSpec(memory_space=pltpu.VMEM)] * 4,
             pl.BlockSpec(memory_space=pl.ANY),
             pl.BlockSpec(memory_space=pl.ANY),
         ],
@@ -394,19 +392,24 @@
             vmem((4 * NC, *chunk), bf16),
             vmem((2, 4 * NC, *chunk), bf16),
             vmem((2 * NC, *chunk), bf16),
-            vmem((8 * Z_FIRST, *chunk), bf16),
+            vmem((2 * NC, *chunk), bf16),
+            vmem((8, 128), i32),
             vmem((16, 8, 128), i32),
-            vmem((16, 128), i32),
-            pltpu.SMEM((8, 128), i32),
-            pltpu.SMEM((16, 128), i32),
+            vmem((32, 128), i32),
+            vmem((1, 256), i32),
+            vmem((2, 256), i32),
+            pltpu.SMEM((1, 256), i32),
+            pltpu.SMEM((2, 256), i32),
+            pltpu.SMEM((32, 128), i32),
             dma((16, NC)),
             dma((4 * NC,)),
             dma((2, 4 * NC)),
             dma((2 * NC,)),
-            dma((8 * Z_FIRST,)),
+            dma((2 * NC,)),
             dma((16,)),
             dma((B_PARTS,)),
             dma,
+            dma((2,)),
             dma,
             dma,
             dma,
@@ -419,7 +422,7 @@
         cost_estimate=pl.CostEstimate(
             flops=2 * 256 * 2 * T * 2 * T * T, bytes_accessed=26 << 20, transcendentals=0
         ),
-    )(meta, a_tiles, b_tiles.reshape(BLOCKS, T, T))
+    )(a_cols.T, b_cols.T, c_cols.T, keep.transpose(2, 1, 0), a_tiles, b_tiles.reshape(BLOCKS, T, T))
 
 
 def solution(mesh):

time: 159 us -> 155 us (0.975)
  other arithmetic: 2.89 us -> 0 us
    unnamed x2 -> x1, local copies, waits for them, and re-layouts: 3.91 us -> 3.16 us
where the time goes in v3:
time: 155 us
  Pallas kernels  151 us (97%)
  local copies, waits for them, and re-layouts  3.16 us (2%)
    pallas_call x1, Pallas kernels, per_device(): pl.pallas_call(kernel, out_shape=jax.ShapeDtypeStruct((2 * ROWS, 2, T, T)...  151 us
    unnamed x1, local copies, waits for them, and re-layouts  3.16 us

profile of v3, /device:TPU:58, one launch (start us, length us, event | category | flops | bytes accessed | tf_op | source)
XLA Modules:
  0.0 154.5 jit_solution(12355438270260935605)
XLA Ops:
  0.0 151.4 %shard_map.64 = bf16[32,2,128,128]{3,2,1,0:T(8,128)(2,1)} custom-call(s32[2,16]{1,0:T(2,128)} %bitcast.9, s32[3,224]{1,0:T(4,128)} %bitcast.7, s32[2,256]{1,0:T(2,128)} %bitcast.8, s32[3,2,256]{2,1,0:T(2,128)} %bitcast.6, bf16[16,2,128,128]{3,2,1,0:T(8,128)(2,1)} %a_ref.1, bf16[672,128,128]{2,1,0:T(8,128)(2,1)} %bitcast.5), custom_call_target="tpu_custom_call" | custom-call | flops 4294967296 | bytes 27262976 | tf_op jit(solution)/shard_map/pallas_call | solution.py:380
  151.4 3.2 %copy.8 = bf16[32,2,128,128]{3,2,1,0:T(8,128)(2,1)} copy(bf16[32,2,128,128]{3,2,1,0:T(8,128)(2,1)} %shard_map.64) | data formatting | bytes 4194304

commit v4 on v3

--- a/solution.py
+++ b/solution.py
@@ -14,6 +14,7 @@
 SB = 3
 BLOCKS = KP * SB
 B_PARTS = 8
+B_EARLY = 4
 
 
 def kernel(
@@ -55,9 +56,9 @@
     ]
     q_own = y * 2 + zl
     own_copy = pltpu.make_async_copy(a_ref, w.at[q_own], sem_own)
-    for copy in b_copies:
+    own_copy.start()
+    for copy in b_copies[:B_EARLY]:
         copy.start()
-    own_copy.start()
 
     barrier = pltpu.get_barrier_semaphore()
     for j in range(1, 16):
@@ -290,12 +291,13 @@
                 add_into(own, c, *both, (rz, (slot,)))
                 write_out(own, kk, c)
 
-    hop0(0)
     for j in range(1, 16):
         remote(mine, land.at[col], send_m, sem_m.at[col], (row, (col + j) % 16)).start()
+    hop0(0)
+    hop0(1)
+    for copy in b_copies[B_EARLY:]:
+        copy.start()
     land[col] = mine[...]
-    hop0(1)
-    hop1(0)
     for j in range(1, 16):
         other = (col + j) % 16
         landed(land.at[other], sem_m.at[other])
@@ -303,6 +305,7 @@
         cols_v[16 * s : 16 * s + 16] = land[:, s, :]
     cols_copy = pltpu.make_async_copy(cols_v, cols_s, sem_cols)
     cols_copy.start()
+    hop1(0)
     for copy in (*words_copies, cols_copy):
         copy.wait()
     own_copy.wait()

time: 155 us -> 153 us (0.987)
  Pallas kernels: 151 us -> 149 us
    pallas_call x1, Pallas kernels: 151 us -> 149 us  [per_device(): pl.pallas_call(kernel, out_shape=jax.ShapeDtypeStruct((2 * ROWS, 2, T, T)...]
where the time goes in v4:
time: 153 us; the launch traced here: 152 us
  Pallas kernels  149 us (97%)
  local copies, waits for them, and re-layouts  3.16 us (2%)
    pallas_call x1, Pallas kernels, per_device(): pl.pallas_call(kernel, out_shape=jax.ShapeDtypeStruct((2 * ROWS, 2, T, T)...  149 us
    unnamed x1, local copies, waits for them, and re-layouts  3.16 us

profile of v4, /device:TPU:58, one launch (start us, length us, event | category | flops | bytes accessed | tf_op | source)
XLA Modules:
  0.0 152.2 jit_solution(6359016659624843117)
XLA Ops:
  0.0 149.0 %shard_map.64 = bf16[32,2,128,128]{3,2,1,0:T(8,128)(2,1)} custom-call(s32[2,16]{1,0:T(2,128)} %bitcast.9, s32[3,224]{1,0:T(4,128)} %bitcast.7, s32[2,256]{1,0:T(2,128)} %bitcast.8, s32[3,2,256]{2,1,0:T(2,128)} %bitcast.6, bf16[16,2,128,128]{3,2,1,0:T(8,128)(2,1)} %a_ref.1, bf16[672,128,128]{2,1,0:T(8,128)(2,1)} %bitcast.5), custom_call_target="tpu_custom_call" | custom-call | flops 4294967296 | bytes 27262976 | tf_op jit(solution)/shard_map/pallas_call | solution.py:383
  149.1 3.2 %copy.8 = bf16[32,2,128,128]{3,2,1,0:T(8,128)(2,1)} copy(bf16[32,2,128,128]{3,2,1,0:T(8,128)(2,1)} %shard_map.64) | data formatting | bytes 4194304

commit v5 on v4

--- a/solution.py
+++ b/solution.py
@@ -18,9 +18,9 @@
 
 
 def kernel(
-    a_cols_ref, b_cols_ref, c_cols_ref, keep_ref, a_ref, b_ref, out_ref,
-    w, bv, rf, rd, rz, rzz, mine, land, cols_v, b_words, c_words, b_words_s, c_words_s, cols_s,
-    sem_a, sem_f, sem_d, sem_z, sem_zz, sem_m, sem_b, sem_own, sem_words, sem_cols, sem_out, send_a, send_p, send_m,
+    a_cols_ref, b_cols_ref, c_cols_ref, keep_ref, a_ref, b_ref, out_ref, far_ref,
+    w, bv, rf, rd, rzz, mine, land, cols_v, b_words, c_words, b_words_s, c_words_s, cols_s,
+    sem_a, sem_f, sem_d, sem_z, sem_zz, sem_m, sem_b, sem_own, sem_words, sem_cols, sem_out, sem_zero, send_a, send_p, send_m,
 ):
     row, col = lax.axis_index("row"), lax.axis_index("col")
     x, zh = row // 2, row % 2
@@ -249,8 +249,8 @@
             landed(rd.at[side, slot], sem_d.at[side, slot])
         return (rd, (0, slot)), (rd, (1, slot))
 
-    def write_out(own, kk, c):
-        pltpu.make_async_copy(chunk(own, c), out_ref.at[pl.ds(kk * ROWS + c * NR, NR)], sem_out).start()
+    def result_rows(ref, kk, c):
+        return ref.at[pl.ds(kk * ROWS + c * NR, NR)]
 
     def middles(c, only_z_first):
         for j in range(2):
@@ -272,24 +272,26 @@
                 own = p_slot(x, 1 - zh, kk)
                 add_into(own, c, *arrived(1 - zh, kk, c))
                 slot = kk * NC + c
-                remote(chunk(own, c), rz.at[slot], send_p, sem_z.at[slot], z_far).start()
+                remote(chunk(own, c), result_rows(far_ref, kk, c), send_p, sem_z.at[slot], z_far).start()
 
     def finish(c):
         for kk in range(2):
             own = p_slot(x, zh, kk)
-            slot = kk * NC + c
+            add_into(own, c, *arrived(zh, kk, c))
+            pltpu.make_async_copy(chunk(own, c), result_rows(out_ref, kk, c), sem_out).start()
 
             @pl.when(z_first(c, kk))
             def _():
-                add_into(own, c, *arrived(zh, kk, c))
-                write_out(own, kk, c)
-
+                for r in range(NR):
+                    for u in range(2):
+                        to = far_ref.at[kk * ROWS + c * NR + r, pl.ds(u, 1)]
+                        pltpu.make_async_copy(bv.at[pl.ds(BLOCKS, 1)], to, sem_zero).start()
+
+    def far_landed(c):
+        for kk in range(2):
             @pl.when(jnp.logical_not(z_first(c, kk)))
             def _():
-                both = arrived(zh, kk, c)
-                landed(rz.at[slot], sem_z.at[slot])
-                add_into(own, c, *both, (rz, (slot,)))
-                write_out(own, kk, c)
+                landed(result_rows(far_ref, kk, c), sem_z.at[kk * NC + c])
 
     for j in range(1, 16):
         remote(mine, land.at[col], send_m, sem_m.at[col], (row, (col + j) % 16)).start()
@@ -364,6 +366,7 @@
         @during(a - 4, NC)
         def _():
             finish(a - 4)
+            far_landed(a - 4)
 
         return carry
 
@@ -373,6 +376,8 @@
     remote(w.at[pl.ds(0, 14)], w.at[pl.ds(0, 14)], send_p, send_p, sibling).wait_send()
     remote(land.at[pl.ds(0, 15)], land.at[pl.ds(0, 15)], send_m, send_m, sibling).wait_send()
     pltpu.make_async_copy(w.at[pl.ds(0, 2)], w.at[pl.ds(0, 2)], sem_out).wait()
+    zeros = w.at[0, pl.ds(0, 8 * NR)]
+    pltpu.make_async_copy(zeros, zeros, sem_zero).wait()
 
 
 def per_device(a_tiles, a_cols, b_tiles, b_cols, c_cols, keep):
@@ -380,21 +385,20 @@
     chunk = (NR, 2, T, T)
     vmem = pltpu.VMEM
     dma = pltpu.SemaphoreType.DMA
-    return pl.pallas_call(
+    own, far = pl.pallas_call(
         kernel,
-        out_shape=jax.ShapeDtypeStruct((2 * ROWS, 2, T, T), bf16),
+        out_shape=[jax.ShapeDtypeStruct((2 * ROWS, 2, T, T), bf16)] * 2,
         in_specs=[
             *[pl.BlockSpec(memory_space=pltpu.VMEM)] * 4,
             pl.BlockSpec(memory_space=pl.ANY),
             pl.BlockSpec(memory_space=pl.ANY),
         ],
-        out_specs=pl.BlockSpec(memory_space=pl.ANY),
+        out_specs=[pl.BlockSpec(memory_space=pl.ANY)] * 2,
         scratch_shapes=[
             vmem((24, ROWS, 2, T, T), bf16),
             vmem((BLOCKS + 1, T, T), bf16),
             vmem((4 * NC, *chunk), bf16),
             vmem((2, 4 * NC, *chunk), bf16),
-            vmem((2 * NC, *chunk), bf16),
             vmem((2 * NC, *chunk), bf16),
             vmem((8, 128), i32),
             vmem((16, 8, 128), i32),
@@ -418,6 +422,7 @@
             dma,
             dma,
             dma,
+            dma,
         ],
         compiler_params=pltpu.CompilerParams(
             collective_id=0, has_side_effects=True, vmem_limit_bytes=63 << 20
@@ -426,6 +431,7 @@
             flops=2 * 256 * 2 * T * 2 * T * T, bytes_accessed=26 << 20, transcendentals=0
         ),
     )(a_cols.T, b_cols.T, c_cols.T, keep.transpose(2, 1, 0), a_tiles, b_tiles.reshape(BLOCKS, T, T))
+    return (own.astype(jnp.float32) + far.astype(jnp.float32)).astype(bf16)
 
 
 def solution(mesh):

time: 153 us -> 154 us (level)
  other arithmetic: 0 us -> 4.65 us
  local copies, waits for them, and re-layouts: 3.16 us -> 0 us
    convert_element_type x0 -> x1, other arithmetic: none -> 4.65 us  [per_device(): return (own.astype(jnp.float32) + far.astype(jnp.float32)).astype(bf16)]
    unnamed x1 -> x0, local copies, waits for them, and re-layouts: 3.16 us -> none
where the time goes in v5:
time: 154 us; the launch traced here: 153 us
  Pallas kernels  149 us (97%)
  other arithmetic  4.65 us (3%)
    pallas_call x1, Pallas kernels, per_device(): pl.pallas_call(kernel, out_shape=[jax.ShapeDtypeStruct((2 * ROWS, 2, T, T...  149 us
    convert_element_type x1, other arithmetic, per_device(): return (own.astype(jnp.float32) + far.astype(jnp.float32)).astype(bf16)  4.65 us

profile of v5, /device:TPU:58, one launch (start us, length us, event | category | flops | bytes accessed | tf_op | source)
XLA Modules:
  0.0 153.2 jit_solution(2982286189863754996)
XLA Ops:
  0.0 148.5 %shard_map.64 = (bf16[32,2,128,128]{3,2,1,0:T(8,128)(2,1)}, bf16[32,2,128,128]{3,2,1,0:T(8,128)(2,1)}) custom-call(s32[2,16]{1,0:T(2,128)} %bitcast.9, s32[3,224]{1,0:T(4,128)} %bitcast.7, s32[2,256]{1,0:T(2,128)} %bitcast.8, s32[3,2,256]{2,1,0:T(2,128)} %bitcast.6, bf16[16,2,128,128]{3,2,1,0:T(8,128)(2,1)} %a_ref.1, bf16[672,128,128]{2,1,0:T(8,128)(2,1)} %bitcast.5), custom_call_target="tpu_custom_call" | custom-call | flops 4294967296 | bytes 27262976 | tf_op jit(solution)/shard_map/pallas_call | solution.py:388
  148.5 4.6 %add_convert_fusion = bf16[32,2,128,128]{3,2,1,0:T(8,128)(2,1)} fusion(bf16[32,2,128,128]{3,2,1,0:T(8,128)(2,1)} %get-tuple-element.8, bf16[32,2,128,128]{3,2,1,0:T(8,128)(2,1)} %get-tuple-element.7), kind=kLoop, calls=%fused_computation | loop fusion | flops 4194304 | bytes 6291456 | tf_op jit(solution)/shard_map/convert_element_type | solution.py:434
